TPU v7x, 32 devices: a whole 2x2x4 slice. The times are simulated.
32 devices in a mesh: groups: 2 (over y), ep: 4 (over z), tp: 4 (over x, core).
Axes of the slice: x: 2, y: 2, z: 4, core: 2. Of those that a mesh axis runs over, the one named last changes fastest.
Arguments:
- queries: bfloat16 [512, 32, 128], P(('groups', 'ep'), 'tp'), parts along dimension 0, may hold values from -8 to 8
- cached_keys: bfloat16 [512, 96, 8, 128], P(('groups', 'ep'), None, 'tp'), parts along dimension 0, may hold values from -8 to 8
- cached_values: bfloat16 [512, 96, 8, 128], P(('groups', 'ep'), None, 'tp'), parts along dimension 0, may hold values from -6 to 6
- lengths: int32 [512], P(('groups', 'ep')), parts along dimension 0, may hold values from 2 to 96, as said below
- expert_ids: int32 [512, 8], P(('groups', 'ep')), parts along dimension 0, may hold values from 0 to 15, all different within a row; in each aligned block of 64 rows (0 to 63, 64 to 127, ...) at most 64 rows name the same one
- latent_proj: bfloat16 [4096, 2048], P('tp'), may hold values from -0.09375 to 0.09375
- latent_gain: float32 [2048], replicated, may hold values from 0.5 to 1.5
- router: bfloat16 [2048, 16], replicated, may hold values from -0.125 to 0.125
- w_gate_up: bfloat16 [16, 2048, 2, 2048], P('ep', None, None, 'tp'), may hold values from -0.125 to 0.125
- w_down: bfloat16 [16, 2048, 2048], P('ep', 'tp'), may hold values from -0.125 to 0.125
- w_up: bfloat16 [2048, 8192], P(None, 'tp'), may hold values from -0.125 to 0.125
Outputs:
- layer_out: bfloat16 [512, 8192], P(('groups', 'ep'), 'tp'), parts along dimension 0
There are 2 independent parts, one for each index of `groups`. A program takes and returns all parts, laid end to end along the dimension named above; an argument that names none is the same for every part. Nothing has to cross between parts.
Inputs may be any that keep to these rules, and one draw needn't show every extreme that they name: `lengths`: every row has 2 or more live positions and some row has all 96.
All inputs are finite; a program needn't handle non-finite values.
Results may differ from a plain program's by a relative error of at most 0.02.
Values may be sent and summed in bfloat16 or wider, within the bound.
A program may use at most 192 MiB of HBM per device.

v0:
```python
import jax
import jax.numpy as jnp
from jax import lax
from jax.sharding import PartitionSpec as P


def attend(queries, cached_keys, cached_values, lengths):
    row_count, head_count, head_depth = queries.shape
    kv_count = cached_keys.shape[2]
    group_size = head_count // kv_count
    query_rows = queries.reshape(row_count, kv_count, group_size, head_depth)
    scores = jnp.einsum(
        "rkgd,rckd->rkgc", query_rows, cached_keys, preferred_element_type=jnp.float32
    ) * head_depth ** (-0.5)
    live_mask = jnp.arange(cached_keys.shape[1], dtype=jnp.int32)[None, :] < lengths[:, None]
    scores = jnp.where(live_mask[:, None, None, :], scores, -1e30)
    attn_probs = jax.nn.softmax(scores, axis=-1).astype(jnp.bfloat16)
    context = jnp.einsum(
        "rkgc,rckd->rkgd", attn_probs, cached_values, preferred_element_type=jnp.float32
    )
    return context.reshape(row_count, head_count * head_depth).astype(jnp.bfloat16)


def expert_math(inbound, w_gate_up, w_down):
    width_dev = w_gate_up.shape[3]
    paired = w_gate_up.reshape(w_gate_up.shape[0], w_gate_up.shape[1], 2 * width_dev)
    gate_up = jnp.einsum("sjnl,jlf->sjnf", inbound, paired, preferred_element_type=jnp.float32)
    hidden = (jax.nn.silu(gate_up[..., :width_dev]) * gate_up[..., width_dev:]).astype(jnp.bfloat16)
    return jnp.einsum("sjnf,jfl->sjnl", hidden, w_down, preferred_element_type=jnp.float32)


def send_back(outputs):
    return lax.all_to_all(outputs, "ep", split_axis=0, concat_axis=0, tiled=True)


def whole_apply(inbound, w_gate_up, w_down):
    return send_back(expert_math(inbound, w_gate_up, w_down))


def route_rows(summed, expert_ids, latent_gain, router, w_gate_up, w_down, applier):
    latent = (
        summed * lax.rsqrt(jnp.mean(summed * summed, axis=-1, keepdims=True) + 1e-06) * latent_gain
    ).astype(jnp.bfloat16)
    logits = jnp.dot(latent, router, preferred_element_type=jnp.float32)
    expert_total = router.shape[1]
    row_count = latent.shape[0]
    chosen = jnp.sum(
        (expert_ids[:, :, None] == jnp.arange(expert_total, dtype=jnp.int32)[None, None, :]).astype(
            jnp.int32
        ),
        axis=1,
    )
    weighted = chosen.astype(jnp.float32) * jax.nn.sigmoid(logits)
    gate_weights = weighted / jnp.sum(weighted, axis=-1, keepdims=True)
    before = jnp.cumsum(chosen, axis=0) - chosen
    slot_index = jnp.arange(row_count, dtype=jnp.int32)[None, :, None]
    slot_map = (before.T[:, None, :] == slot_index) & (chosen.T[:, None, :] > 0)
    outgoing = jnp.einsum(
        "ecr,rl->ecl", slot_map.astype(jnp.bfloat16), latent, preferred_element_type=jnp.float32
    ).astype(jnp.bfloat16)
    local_count = w_gate_up.shape[0]
    outgoing = outgoing.reshape(
        expert_total // local_count, local_count, row_count, latent.shape[1]
    )
    returned_rows = applier(
        lax.all_to_all(outgoing, "ep", split_axis=0, concat_axis=0, tiled=True), w_gate_up, w_down
    )
    returned_rows = returned_rows.reshape(expert_total, row_count, latent.shape[1])
    blend_map = slot_map.astype(jnp.float32) * gate_weights.T[:, None, :]
    return jnp.einsum(
        "ecr,ecl->rl",
        blend_map,
        returned_rows,
        preferred_element_type=jnp.float32,
        precision=lax.Precision.HIGHEST,
    )


def body(
    queries,
    cached_keys,
    cached_values,
    lengths,
    expert_ids,
    latent_proj,
    latent_gain,
    router,
    w_gate_up,
    w_down,
    w_up,
):
    context = attend(queries, cached_keys, cached_values, lengths)
    partial_value = jnp.dot(context, latent_proj, preferred_element_type=jnp.float32)
    summed = lax.psum(partial_value, "tp")
    mixture = route_rows(summed, expert_ids, latent_gain, router, w_gate_up, w_down, whole_apply)
    combined = lax.psum(mixture, "tp").astype(jnp.bfloat16)
    return jnp.dot(combined, w_up, preferred_element_type=jnp.float32).astype(jnp.bfloat16)


def solution(mesh):
    return jax.shard_map(
        body,
        mesh=mesh,
        in_specs=(
            P(("groups", "ep"), "tp", None),
            P(("groups", "ep"), None, "tp", None),
            P(("groups", "ep"), None, "tp", None),
            P(("groups", "ep")),
            P(("groups", "ep"), None),
            P("tp", None),
            P(),
            P(),
            P("ep", None, None, "tp"),
            P("ep", "tp", None),
            P(None, "tp"),
        ),
        out_specs=P(("groups", "ep"), "tp"),
        check_vma=False,
    )
```

profile of v0, /device:TPU:0, one launch (start us, length us, event | category | flops | bytes accessed | tf_op | source)
XLA Modules:
  0.0 402.4 jit_solution(11112160890481811660)
XLA Ops:
  6.5 0.0 copy-start
  6.5 0.0 all-reduce.3.cloned.1.call-start
  6.5 0.9 iota_compare_fusion.2
  7.4 4.6 %fusion.51 = (f32[64,2,4]{2,1,0:T(2,128)}, f32[64,2,4,96]{3,2,1,0:T(4,128)S(1)}) fusion(bf16[64,2,4,128]{3,2,1,0:T(4,128)(2,1)} %bitcast.38, bf16[64,96,2,128]{3,2,1,0:T(2,128)(2,1)} %param.12, pred[64,96]{1,0:T(8,128)(4,1)S(1)} %iota_compare_fusion.2), kind=kOutput, calls=%fused_computation.52 | convolution fusion | flops 12779615 | bytes 3481600 | tf_op jit(solution)/shard_map/sub | solution.py:17
  12.0 0.0 copy-done
  12.0 1.8 fusion.27
  13.8 0.0 copy-start.5
  13.8 0.0 copy-start.4
  13.9 0.1 convert_element_type.41
  13.9 3.8 fusion.55
  17.8 0.0 all-reduce.3.cloned.1.call-update
  17.8 0.0 copy-done.5
  17.8 0.1 copy.33
  17.9 0.1 reduce_window_sum.11
  18.0 0.1 copy.35
  18.1 35.8 %all-reduce.3.cloned.1.call-done = f32[64,2048]{1,0:T(8,128)} async-done(((f32[64,2048]{1,0:T(8,128)}), f32[64,2048]{1,0:T(8,128)}) %all-reduce.3.cloned.1.call-update) | async-done | bytes 524304 | tf_op jit(solution)/shard_map/psum | solution.py:94
  53.8 1.2 multiply_reduce_fusion
  55.0 0.0 copy-done.4
  55.0 4.5 %convolution_convert_fusion = bf16[16,64,2048]{2,1,0:T(8,128)(2,1)} fusion(s32[16,64]{1,0:T(8,128)S(1)} %copy.35, pred[16,64]{1,0:T(8,128)(4,1)S(1)} %compare_bitcast_fusion, f32[64,2048]{1,0:T(8,128)} %all-reduce.3.cloned.1.call-done, f32[2048]{0:T(1024)S(1)} %copy-done.4, f32[64]{0:T(128)S(1)} %add_rsqrt_fusion), kind=kOutput, calls=%fused_computation.7 | convolution fusion | flops 271056896 | bytes 4732160 | tf_op jit(solution)/shard_map/ecr,rl->ecl/dot_general | solution.py:58
  59.5 4.9 %all-to-all-start = ((bf16[4,4,64,2048]{3,2,1,0:T(8,128)(2,1)}), bf16[4,4,64,2048]{3,2,1,0:T(8,128)(2,1)}, u32[]{:S(2)}, u32[]{:S(2)}) async-start(bf16[4,4,64,2048]{3,2,1,0:T(8,128)(2,1)} %bitcast.37), calls=%async_computation | async-start | bytes 8388608 | tf_op jit(solution)/shard_map/all_to_all | solution.py:66
  64.4 27.3 %reshape.53 = bf16[4,2048,1024,1]{2,1,0,3:T(8,128)(2,1)} reshape(bf16[4,2048,2,512]{3,2,1,0:T(2,128)(2,1)} %param.19) | data formatting | bytes 33554432 | tf_op jit(solution)/shard_map/reshape | solution.py:26
  91.7 65.0 %all-to-all-done = bf16[4,4,64,2048]{3,2,1,0:T(8,128)(2,1)} async-done(((bf16[4,4,64,2048]{3,2,1,0:T(8,128)(2,1)}), bf16[4,4,64,2048]{3,2,1,0:T(8,128)(2,1)}, u32[]{:S(2)}, u32[]{:S(2)}) %all-to-all-start) | async-done | bytes 4194336 | tf_op jit(solution)/shard_map/all_to_all | solution.py:66
  156.7 9.4 %fusion.13 = f32[4,4,64,1024]{3,2,0,1:T(8,128)S(1)} fusion(bf16[4,2048,1024,1]{2,1,0,3:T(8,128)(2,1)} %reshape.53, bf16[4,4,64,2048]{3,2,1,0:T(8,128)(2,1)} %all-to-all-done), kind=kOutput, calls=%fused_computation.14 | convolution fusion | flops 4294967296 | bytes 25165824 | tf_op jit(solution)/shard_map/sjnl,jlf->sjnf/dot_general | solution.py:27
  166.1 5.9 %fusion.5 = f32[4,4,64,2048]{3,2,0,1:T(8,128)S(1)} fusion(bf16[4,512,2048]{2,1,0:T(8,128)(2,1)} %param.20, f32[4,4,64,1024]{3,2,0,1:T(8,128)S(1)} %fusion.13), kind=kOutput, calls=%fused_computation.5 | convolution fusion | flops 2150629376 | bytes 20971520 | tf_op jit(solution)/shard_map/sjnf,jfl->sjnl/dot_general | solution.py:29
  172.0 3.8 copy.40
  175.8 0.0 copy-start.2
  175.8 0.0 copy-start.3
  175.8 5.8 %all-to-all-start.1 = ((f32[4,4,64,2048]{3,2,1,0:T(8,128)}), f32[4,4,64,2048]{3,2,1,0:T(8,128)}, u32[]{:S(2)}, u32[]{:S(2)}) async-start(f32[4,4,64,2048]{3,2,1,0:T(8,128)} %copy.40), calls=%async_computation.1 | async-start | bytes 16777216 | tf_op jit(solution)/shard_map/all_to_all | solution.py:33
  181.6 0.0 copy-done.2
  181.6 0.0 copy-done.3
  181.6 0.3 fusion.52
  181.9 182.2 %all-to-all-done.1 = f32[4,4,64,2048]{3,2,1,0:T(8,128)} async-done(((f32[4,4,64,2048]{3,2,1,0:T(8,128)}), f32[4,4,64,2048]{3,2,1,0:T(8,128)}, u32[]{:S(2)}, u32[]{:S(2)}) %all-to-all-start.1) | async-done | bytes 8388640 | tf_op jit(solution)/shard_map/all_to_all | solution.py:33
  364.1 8.8 %convolution_bitcast_fusion = f32[64,2048]{1,0:T(8,128)} fusion(f32[16,64,2048]{2,1,0:T(8,128)} %bitcast.11, f32[16,64]{1,0:T(8,128)S(1)} %divide_bitcast_fusion, s32[16,64]{1,0:T(8,128)S(1)} %copy.35, pred[16,64]{1,0:T(8,128)(4,1)S(1)} %compare_bitcast_fusion), kind=kOutput, calls=%fused_computation.12 | convolution fusion | flops 1610809344 | bytes 8922112 | tf_op jit(solution)/shard_map/ecr,ecl->rl/dot_general | solution.py:70
  372.9 0.0 copy-start.1
  373.0 16.9 %all-reduce.4 = bf16[64,2048]{1,0:T(8,128)(2,1)S(1)} all-reduce(f32[64,2048]{1,0:T(8,128)} %convolution_bitcast_fusion), channel_id=1, replica_groups=mesh['groups'=2,'ep'=4,'tp'=4] {'tp'}, use_global_device_ids=true, to_apply=%region_7.8 | all-reduce | flops 131072 | bytes 786432 | tf_op jit(solution)/shard_map/psum | solution.py:96
  389.9 5.7 %convolution_convert_fusion.1 = bf16[64,2048]{1,0:T(8,128)(2,1)} fusion(bf16[2048,2048]{1,0:T(8,128)(2,1)} %param.21, bf16[64,2048]{1,0:T(8,128)(2,1)S(1)} %all-reduce.4), kind=kOutput, calls=%fused_computation.13 | convolution fusion | flops 537001984 | bytes 8912896 | tf_op jit(solution)/shard_map/dot_general | solution.py:97
  395.5 0.0 copy-done.1
  (5 shorter events, 0.0 us)
Async XLA Ops:
  6.5 5.5 %copy-start = (bf16[64,96,2,128]{3,2,1,0:T(2,128)(2,1)S(1)}, bf16[64,96,2,128]{3,2,1,0:T(2,128)(2,1)}, u32[]{:S(2)}) copy-start(bf16[64,96,2,128]{3,2,1,0:T(2,128)(2,1)} %param.13) | copy-start | bytes 9437188
  6.5 47.3 %all-reduce.3.cloned.1.call-start = ((), (), s32[]{:S(2)}) async-start(), calls=%async_computation.2 | async-start | bytes 1048576 | tf_op jit(solution)/shard_map/psum | solution.py:94
  13.8 3.9 copy-start.5
  13.8 41.2 %copy-start.4 = (f32[2048]{0:T(1024)S(1)}, f32[2048]{0:T(1024)}, u32[]{:S(2)}) copy-start(f32[2048]{0:T(1024)} %param.17) | copy-start | bytes 24580
  59.5 97.2 %all-to-all-start = ((bf16[4,4,64,2048]{3,2,1,0:T(8,128)(2,1)}), bf16[4,4,64,2048]{3,2,1,0:T(8,128)(2,1)}, u32[]{:S(2)}, u32[]{:S(2)}) async-start(bf16[4,4,64,2048]{3,2,1,0:T(8,128)(2,1)} %bitcast.37), calls=%async_computation | async-start | bytes 8388608 | tf_op jit(solution)/shard_map/all_to_all | solution.py:66
  175.8 5.8 %copy-start.2 = (f32[64,2048]{1,0:T(8,128)S(1)}, f32[64,2048]{1,0:T(8,128)}, u32[]{:S(2)}) copy-start(f32[64,2048]{1,0:T(8,128)} %all-reduce.3.cloned.1.call-done) | copy-start | bytes 1572868
  175.8 5.8 %copy-start.3 = (bf16[2048,16]{0,1:T(8,128)(2,1)S(1)}, bf16[2048,16]{0,1:T(8,128)(2,1)}, u32[]{:S(2)}) copy-start(bf16[2048,16]{0,1:T(8,128)(2,1)} %param.18) | copy-start | bytes 196612
  175.8 188.4 %all-to-all-start.1 = ((f32[4,4,64,2048]{3,2,1,0:T(8,128)}), f32[4,4,64,2048]{3,2,1,0:T(8,128)}, u32[]{:S(2)}, u32[]{:S(2)}) async-start(f32[4,4,64,2048]{3,2,1,0:T(8,128)} %copy.40), calls=%async_computation.1 | async-start | bytes 16777216 | tf_op jit(solution)/shard_map/all_to_all | solution.py:33
  372.9 22.6 %copy-start.1 = (bf16[64,96,2,128]{3,2,1,0:T(2,128)(2,1)S(1)}, bf16[64,96,2,128]{3,2,1,0:T(2,128)(2,1)}, u32[]{:S(2)}) copy-start(bf16[64,96,2,128]{3,2,1,0:T(2,128)(2,1)} %param.13) | copy-start | bytes 9437188
Sparse Core Ops, SparseCore 0:
  17.9 35.8 all-reduce.2
where the time goes:
time: 404 us; the launch traced here: 402 us
  waiting for transfers between devices  283 us (70%)
  matrix products  44.7 us (11%)
  local copies, waits for them, and re-layouts  31.4 us (8%)
  blocking collectives  16.9 us (4%)
  between operations  13.5 us (3%)
  starting transfers between devices  10.6 us (3%)
    all_to_all x1, waiting for transfers between devices, send_back(): lax.all_to_all(outputs, 'ep', split_axis=0, concat_axis=0, tiled=True)  182 us
    all_to_all x1, waiting for transfers between devices, route_rows(): lax.all_to_all(outgoing, 'ep', split_axis=0, concat_axis=0, tiled=True)  65 us
    psum x1, waiting for transfers between devices, body(): summed = lax.psum(partial_value, 'tp')  35.8 us
    reshape x1, local copies, waits for them, and re-layouts, expert_math(): w_gate_up.reshape(w_gate_up.shape[0], w_gate_up.shape[1], 2 * width_dev)  27.3 us
    psum x1, blocking collectives, body(): combined = lax.psum(mixture, 'tp').astype(jnp.bfloat16)  16.9 us
    dot_general x1, matrix products, expert_math(): jnp.einsum('sjnl,jlf->sjnf', inbound, paired, preferred_element_type=jnp....  9.39 us
    dot_general x1, matrix products, route_rows(): jnp.einsum('ecr,ecl->rl', blend_map, returned_rows, preferred_element_typ...  8.8 us
  transfers between devices with their start and end apart: 3, of which 3 were waited for; matrix products, arithmetic and copies ran while one was open for 7% of the time, Pallas kernels for 0%

commit v1 on v0

v1 whole, which is shorter than its diff:
```python
import jax
import jax.numpy as jnp
from jax import lax
from jax.sharding import PartitionSpec as P


def attend(queries, cached_keys, cached_values, lengths):
    row_count, head_count, head_depth = queries.shape
    kv_count = cached_keys.shape[2]
    group_size = head_count // kv_count
    query_rows = queries.reshape(row_count, kv_count, group_size, head_depth)
    scores = jnp.einsum(
        "rkgd,rckd->rkgc", query_rows, cached_keys, preferred_element_type=jnp.float32
    ) * head_depth ** (-0.5)
    live_mask = jnp.arange(cached_keys.shape[1], dtype=jnp.int32)[None, :] < lengths[:, None]
    scores = jnp.where(live_mask[:, None, None, :], scores, -1e30)
    attn_probs = jax.nn.softmax(scores, axis=-1).astype(jnp.bfloat16)
    context = jnp.einsum(
        "rkgc,rckd->rkgd", attn_probs, cached_values, preferred_element_type=jnp.float32
    )
    return context.reshape(row_count, head_count * head_depth).astype(jnp.bfloat16)


def body(queries, cached_keys, cached_values, lengths, expert_ids, latent_proj, latent_gain, router, w_gate_up, w_down, w_up):
    expert_total = router.shape[1]
    local_count, latent_width, _, hidden_dev = w_gate_up.shape
    all_ids = lax.all_gather(expert_ids, "ep", axis=0, tiled=True)
    context = attend(queries, cached_keys, cached_values, lengths)
    partial_value = jnp.dot(context, latent_proj, preferred_element_type=jnp.float32)
    summed = lax.psum_scatter(partial_value, "tp", scatter_dimension=0, tiled=True)
    latent = (
        summed * lax.rsqrt(jnp.mean(summed * summed, axis=-1, keepdims=True) + 1e-06) * latent_gain
    ).astype(jnp.bfloat16)
    latent = lax.all_gather(latent, ("ep", "tp"), axis=0, tiled=True)
    logits = jnp.dot(latent, router, preferred_element_type=jnp.float32)
    chosen = jnp.sum(
        (all_ids[:, :, None] == jnp.arange(expert_total, dtype=jnp.int32)[None, None, :]).astype(jnp.float32),
        axis=1,
    )
    weighted = chosen * jax.nn.sigmoid(logits)
    gate_weights = weighted / jnp.sum(weighted, axis=-1, keepdims=True)
    mine = lax.dynamic_slice_in_dim(gate_weights, lax.axis_index("ep") * local_count, local_count, 1)
    paired = w_gate_up.reshape(local_count, latent_width, 2 * hidden_dev)
    hidden = []
    for e in range(local_count):
        gate_up = jnp.dot(latent, paired[e], preferred_element_type=jnp.float32)
        gate, up = gate_up[:, :hidden_dev], gate_up[:, hidden_dev:]
        hidden.append((jax.nn.silu(gate) * up * mine[:, e : e + 1]).astype(jnp.bfloat16))
    mixture = jnp.dot(
        jnp.concatenate(hidden, axis=1),
        w_down.reshape(local_count * hidden_dev, latent_width),
        preferred_element_type=jnp.float32,
    ).astype(jnp.bfloat16)
    part = lax.psum_scatter(mixture, ("ep", "tp"), scatter_dimension=0, tiled=True)
    combined = lax.all_gather(part, "tp", axis=0, tiled=True)
    return jnp.dot(combined, w_up, preferred_element_type=jnp.float32).astype(jnp.bfloat16)


def solution(mesh):
    return jax.shard_map(
        body,
        mesh=mesh,
        in_specs=(
            P(("groups", "ep"), "tp", None),
            P(("groups", "ep"), None, "tp", None),
            P(("groups", "ep"), None, "tp", None),
            P(("groups", "ep")),
            P(("groups", "ep"), None),
            P("tp", None),
            P(),
            P(),
            P("ep", None, None, "tp"),
            P("ep", "tp", None),
            P(None, "tp"),
        ),
        out_specs=P(("groups", "ep"), "tp"),
        check_vma=False,
    )
```

time: 404 us -> 181 us (0.45)
  waiting for transfers between devices: 283 us -> 82.1 us
  matrix products: 44.7 us -> 28.6 us
  starting transfers between devices: 10.6 us -> 0.09 us
    all_to_all x2 -> x0, waiting for transfers between devices: 247 us -> none  [the longest x1 182 us: send_back(): lax.all_to_all(outputs, 'ep', split_axis=0, concat_axis=0, tiled=True)]
    reduce_scatter x0 -> x2, waiting for transfers between devices: none -> 82 us  [the longest x1 57.6 us: body(): lax.psum_scatter(mixture, ('ep', 'tp'), scatter_dimension=0, tiled=True)]
    psum x1 -> x0, waiting for transfers between devices: 35.8 us -> none  [body(): summed = lax.psum(partial_value, 'tp')]
    reshape x1 -> x0, local copies, waits for them, and re-layouts: 27.3 us -> none  [expert_math(): w_gate_up.reshape(w_gate_up.shape[0], w_gate_up.shape[1], 2 * width_dev)]
    all_gather x0 -> x2, blocking collectives: none -> 19.5 us  [the longest x1 13.4 us: body(): all_ids = lax.all_gather(expert_ids, 'ep', axis=0, tiled=True)]
    psum x1 -> x0, blocking collectives: 16.9 us -> none  [body(): combined = lax.psum(mixture, 'tp').astype(jnp.bfloat16)]
    unnamed x12 -> x31, local copies, waits for them, and re-layouts: 0.02 us -> 16.7 us
    dot_general x5 -> x6, matrix products: 28.8 us -> 12.7 us  [the longest x4 7.64 us: body(): gate_up = jnp.dot(latent, paired[e], preferred_element_type=jnp.float32)]
  transfers between devices with their start and end apart: 3 -> 3, of which waited for: 3 -> 2; matrix products, arithmetic and copies ran while one was open for 7% -> 17% of each run, Pallas kernels for 0% -> 0%
where the time goes in v1:
time: 181 us
  waiting for transfers between devices  82.1 us (45%)
  local copies, waits for them, and re-layouts  32.8 us (18%)
  matrix products  28.6 us (16%)
  blocking collectives  19.5 us (11%)
  between operations  13.3 us (7%)
  other arithmetic  4.2 us (2%)
    reduce_scatter x1, waiting for transfers between devices, body(): lax.psum_scatter(mixture, ('ep', 'tp'), scatter_dimension=0, tiled=True)  57.6 us
    reduce_scatter x1, waiting for transfers between devices, body(): lax.psum_scatter(partial_value, 'tp', scatter_dimension=0, tiled=True)  24.4 us
    unnamed x31, local copies, waits for them, and re-layouts  16.7 us
    slice x1, local copies, waits for them, and re-layouts, body(): gate_up = jnp.dot(latent, paired[e], preferred_element_type=jnp.float32)  16 us
    all_gather x1, blocking collectives, body(): all_ids = lax.all_gather(expert_ids, 'ep', axis=0, tiled=True)  13.4 us
    dot_general x4, matrix products, body(): gate_up = jnp.dot(latent, paired[e], preferred_element_type=jnp.float32)  7.64 us
    all_gather x1, blocking collectives, body(): combined = lax.all_gather(part, 'tp', axis=0, tiled=True)  6.12 us
    dot_general x1, matrix products, body(): jnp.dot(combined, w_up, preferred_element_type=jnp.float32)  5.66 us
  transfers between devices with their start and end apart: 3, of which 2 were waited for; matrix products, arithmetic and copies ran while one was open for 17% of the time, Pallas kernels for 0%

profile of v1, /device:TPU:0, one launch (start us, length us, event | category | flops | bytes accessed | tf_op | source)
XLA Modules:
  0.0 180.6 jit_solution(7262274289828360161)
XLA Ops:
  6.5 0.0 copy-start
  6.5 0.0 reduce-scatter.3.cloned.1.call-start
  6.5 0.9 iota_compare_fusion.1
  7.4 4.6 %fusion.39 = (f32[64,2,4]{2,1,0:T(2,128)}, f32[64,2,4,96]{3,2,1,0:T(4,128)S(1)}) fusion(bf16[64,2,4,128]{3,2,1,0:T(4,128)(2,1)} %bitcast.53, bf16[64,96,2,128]{3,2,1,0:T(2,128)(2,1)} %param.12, pred[64,96]{1,0:T(8,128)(4,1)S(1)} %iota_compare_fusion.1), kind=kOutput, calls=%fused_computation.48 | convolution fusion | flops 12779615 | bytes 3481600 | tf_op jit(solution)/shard_map/sub | solution.py:17
  12.0 0.0 copy-done
  12.0 1.8 %fusion.13 = bf16[64,2,4,128]{3,2,1,0:T(4,128)(2,1)S(1)} fusion(bf16[64,96,2,128]{3,2,1,0:T(2,128)(2,1)S(1)} %copy-done, f32[64,2,4,96]{3,2,1,0:T(4,128)S(1)} %get-tuple-element.14, f32[64,2,4]{2,1,0:T(2,128)} %get-tuple-element.13), kind=kOutput, calls=%fused_computation.11 | convolution fusion | flops 12746752 | bytes 3475456 | tf_op jit(solution)/shard_map/rkgc,rckd->rkgd/dot_general | solution.py:18
  13.8 0.0 copy-start.9
  13.8 0.1 convert_element_type.35
  13.9 3.8 %fusion.43 = f32[64,2048]{1,0:T(8,128)} fusion(bf16[64,1024]{1,0:T(8,128)(2,1)S(1)} %convert_element_type.35, bf16[1024,2048]{1,0:T(8,128)(2,1)} %param.16), kind=kOutput, calls=%fused_computation.50 | convolution fusion | flops 268435456 | bytes 4849664 | tf_op jit(solution)/shard_map/dot_general | solution.py:29
  17.8 0.0 reduce-scatter.3.cloned.1.call-update
  17.8 0.0 all-gather.3.cloned.1.call-start
  17.8 24.4 %reduce-scatter.3.cloned.1.call-done = f32[16,2048]{1,0:T(8,128)} async-done(((f32[64,2048]{1,0:T(8,128)}), f32[16,2048]{1,0:T(8,128)}) %reduce-scatter.3.cloned.1.call-update) | async-done | bytes 131088 | tf_op jit(solution)/shard_map/reduce_scatter | solution.py:30
  42.3 1.0 multiply_reduce_fusion
  43.3 0.0 copy-done.9
  43.3 1.6 multiply_convert_fusion
  44.9 0.0 all-gather.3.cloned.1.call-update
  45.0 0.0 reduce-scatter.5.cloned.1.call-start
  45.0 16.0 %fusion.37 = (bf16[1,2048,2,512]{3,2,1,0:T(2,128)(2,1)}, bf16[1,2048,2,512]{3,2,1,0:T(2,128)(2,1)}, bf16[1,2048,2,512]{3,2,1,0:T(2,128)(2,1)S(1)}, bf16[1,2048,2,512]{3,2,1,0:T(2,128)(2,1)}) fusion(bf16[4,2048,2,512]{3,2,1,0:T(2,128)(2,1)} %param.19), kind=kLoop, calls=%fused_computation.46 | loop fusion | bytes 33554432 | tf_op jit(solution)/shard_map/slice | solution.py:46
  61.0 0.0 copy-start.10
  61.0 3.1 %copy.28 = bf16[256,8,2,512]{3,1,2,0:T(8,128)(2,1)} copy(bf16[256,8,2,512]{3,2,1,0:T(2,128)(2,1)S(1)} %bitcast.40) | data formatting | bytes 8388608
  64.1 0.0 copy-done.10
  64.2 13.4 %all-gather = s32[4,64,8]{1,2,0:T(8,128)S(1)} all-gather(s32[1,64,8]{1,2,0:T(8,128)S(1)} %bitcast.49), channel_id=1, replica_groups=mesh['groups'=2,'ep'=4,'tp'=4] {'ep'}, dimensions={0}, use_global_device_ids=true | all-gather | bytes 10240 | tf_op jit(solution)/shard_map/all_gather | solution.py:27
  77.5 0.1 reshape.50
  77.6 0.0 copy-start.3
  77.6 5.5 %copy.27 = bf16[256,8,2,512]{3,1,2,0:T(8,128)(2,1)} copy(bf16[256,8,2,512]{3,2,1,0:T(2,128)(2,1)} %bitcast.39) | data formatting | bytes 8388608
  83.1 0.0 copy-done.3
  83.1 0.0 copy-start.2
  83.1 3.1 %copy.26 = bf16[256,8,2,512]{3,1,2,0:T(8,128)(2,1)} copy(bf16[256,8,2,512]{3,2,1,0:T(2,128)(2,1)S(1)} %bitcast.38) | data formatting | bytes 8388608
  86.3 0.0 copy-done.2
  86.3 0.0 copy-start.8
  86.3 3.2 %copy.25 = bf16[256,8,2,512]{3,1,2,0:T(8,128)(2,1)} copy(bf16[256,8,2,512]{3,2,1,0:T(2,128)(2,1)S(1)} %bitcast.37) | data formatting | bytes 8388608
  89.4 0.0 all-gather.3.cloned.1.call-done
  89.5 0.0 copy-done.8
  89.5 0.0 copy-start.6
  89.5 0.0 copy-start.7
  89.5 1.8 fusion.40
  91.3 3.8 %fusion.47 = f32[256,1024]{1,0:T(8,128)S(1)} fusion(bf16[256,2048]{1,0:T(8,128)(2,1)} %all-gather.3.cloned.1.call-done, bf16[2048,1024]{1,0:T(8,128)(2,1)} %bitcast.41), kind=kOutput, calls=%fused_computation.54 | convolution fusion | flops 1073741824 | bytes 6291456 | tf_op jit(solution)/shard_map/dot_general | solution.py:46
  95.1 0.0 copy-done.6
  95.1 0.0 copy-done.7
  95.1 0.0 copy-start.4
  95.2 0.0 slice-start
  95.2 1.3 fusion.46
  96.5 0.3 fusion.28
  96.8 0.0 copy-start.5
  96.8 0.5 copy-done.4
  97.3 0.0 slice-start.1
  97.3 1.3 fusion.45
  98.6 1.1 copy-done.5
  99.7 1.3 fusion.44
  101.0 0.3 fusion.32
  101.3 0.0 slice-done
  101.3 0.0 slice-done.1
  101.4 3.3 %convolution_convert_fusion = bf16[256,2048]{1,0:T(8,128)(2,1)} fusion(bf16[2048,2048]{1,0:T(8,128)(2,1)S(1)} %bitcast.52, bf16[256,512]{1,0:T(8,128)(2,1)S(1)} %get-tuple-element.17, bf16[256,512]{1,0:T(8,128)(2,1)S(1)} %get-tuple-element.18, bf16[256,512]{1,0:T(8,128)(2,1)S(1)} %get-tuple-element.19, bf16[256,512]{1,0:T(8,128)(2,1)S(1)} %get-tuple-element.20), kind=kOutput, calls=%fused_computation.5 | convolution fusion | flops 2152202240 | bytes 10485760 | tf_op jit(solution)/shard_map/dot_general | solution.py:49
  104.7 0.0 reduce-scatter.5.cloned.1.call-update
  104.7 57.6 %reduce-scatter.5.cloned.1.call-done = bf16[16,2048]{1,0:T(8,128)(2,1)} async-done(((bf16[256,2048]{1,0:T(8,128)(2,1)}), bf16[16,2048]{1,0:T(8,128)(2,1)}) %reduce-scatter.5.cloned.1.call-update) | async-done | bytes 65552 | tf_op jit(solution)/shard_map/reduce_scatter | solution.py:54
  162.3 0.0 copy-start.1
  162.3 6.1 %all_gather.11 = bf16[64,2048]{1,0:T(8,128)(2,1)S(1)} all-gather(bf16[16,2048]{1,0:T(8,128)(2,1)} %reduce-scatter.5.cloned.1.call-done), channel_id=1, replica_groups=mesh['groups'=2,'ep'=4,'tp'=4] {'tp'}, dimensions={0}, use_global_device_ids=true | all-gather | bytes 327680 | tf_op jit(solution)/shard_map/all_gather | solution.py:55
  168.4 5.7 %convolution_convert_fusion.1 = bf16[64,2048]{1,0:T(8,128)(2,1)} fusion(bf16[64,2048]{1,0:T(8,128)(2,1)S(1)} %all_gather.11, bf16[2048,2048]{1,0:T(8,128)(2,1)} %param.21), kind=kOutput, calls=%fused_computation.6 | convolution fusion | flops 537001984 | bytes 8912896 | tf_op jit(solution)/shard_map/dot_general | solution.py:56
  174.1 0.0 copy-done.1
  (6 shorter events, 0.1 us)
Async XLA Ops:
  6.5 5.5 %copy-start = (bf16[64,96,2,128]{3,2,1,0:T(2,128)(2,1)S(1)}, bf16[64,96,2,128]{3,2,1,0:T(2,128)(2,1)}, u32[]{:S(2)}) copy-start(bf16[64,96,2,128]{3,2,1,0:T(2,128)(2,1)} %param.13) | copy-start | bytes 9437188
  6.5 35.7 %reduce-scatter.3.cloned.1.call-start = ((), (), s32[]{:S(2)}) async-start(), calls=%async_computation.2 | async-start | bytes 655360 | tf_op jit(solution)/shard_map/reduce_scatter | solution.py:30
  13.8 29.5 %copy-start.9 = (f32[2048]{0:T(1024)S(1)}, f32[2048]{0:T(1024)}, u32[]{:S(2)}) copy-start(f32[2048]{0:T(1024)} %param.17) | copy-start | bytes 24580
  17.8 71.7 %all-gather.3.cloned.1.call-start = ((), (), s32[]{:S(2)}) async-start(), calls=%async_computation.3 | async-start | bytes 1114112 | tf_op jit(solution)/shard_map/all_gather | solution.py:34
  45.0 117.3 %reduce-scatter.5.cloned.1.call-start = ((), (), s32[]{:S(2)}) async-start(), calls=%async_computation.4 | async-start | bytes 1114112 | tf_op jit(solution)/shard_map/reduce_scatter | solution.py:54
  61.0 3.1 %copy-start.10 = (s32[64,8]{0,1:T(8,128)S(1)}, s32[64,8]{0,1:T(8,128)}, u32[]{:S(2)}) copy-start(s32[64,8]{0,1:T(8,128)} %param.15) | copy-start | bytes 6148
  77.6 5.5 %copy-start.3 = (bf16[1,2048,2,512]{3,2,1,0:T(2,128)(2,1)S(1)}, bf16[1,2048,2,512]{3,2,1,0:T(2,128)(2,1)}, u32[]{:S(2)}) copy-start(bf16[1,2048,2,512]{3,2,1,0:T(2,128)(2,1)} %get-tuple-element.6) | copy-start | bytes 12582916
  83.1 3.1 %copy-start.2 = (bf16[1,2048,2,512]{3,2,1,0:T(2,128)(2,1)S(1)}, bf16[1,2048,2,512]{3,2,1,0:T(2,128)(2,1)}, u32[]{:S(2)}) copy-start(bf16[1,2048,2,512]{3,2,1,0:T(2,128)(2,1)} %get-tuple-element.5) | copy-start | bytes 12582916
  86.3 3.2 %copy-start.8 = (bf16[2048,16]{0,1:T(8,128)(2,1)S(1)}, bf16[2048,16]{0,1:T(8,128)(2,1)}, u32[]{:S(2)}) copy-start(bf16[2048,16]{0,1:T(8,128)(2,1)} %param.18) | copy-start | bytes 196612
  89.5 5.6 %copy-start.6 = (bf16[256,8,2,512]{3,1,2,0:T(8,128)(2,1)S(1)}, bf16[256,8,2,512]{3,1,2,0:T(8,128)(2,1)}, u32[]{:S(2)}) copy-start(bf16[256,8,2,512]{3,1,2,0:T(8,128)(2,1)} %copy.27) | copy-start | bytes 12582916
  89.5 5.6 %copy-start.7 = (bf16[256,2048]{1,0:T(8,128)(2,1)S(1)}, bf16[256,2048]{1,0:T(8,128)(2,1)}, u32[]{:S(2)}) copy-start(bf16[256,2048]{1,0:T(8,128)(2,1)} %all-gather.3.cloned.1.call-done) | copy-start | bytes 3145732
  95.1 2.2 %copy-start.4 = (bf16[256,8,2,512]{3,1,2,0:T(8,128)(2,1)S(1)}, bf16[256,8,2,512]{3,1,2,0:T(8,128)(2,1)}, u32[]{:S(2)}) copy-start(bf16[256,8,2,512]{3,1,2,0:T(8,128)(2,1)} %copy.26) | copy-start | bytes 12582916
  95.2 6.2 %slice-start = ((s8[8388608]{0:T(1024)(128)(4,1)}), s8[4194304]{0:T(1024)(128)(4,1)S(1)}, s32[]{:S(2)}) async-start(s8[8388608]{0:T(1024)(128)(4,1)} %bitcast.50), calls=%async_computation.5 | async-start | bytes 8388608
  96.8 2.9 %copy-start.5 = (bf16[256,8,2,512]{3,1,2,0:T(8,128)(2,1)S(1)}, bf16[256,8,2,512]{3,1,2,0:T(8,128)(2,1)}, u32[]{:S(2)}) copy-start(bf16[256,8,2,512]{3,1,2,0:T(8,128)(2,1)} %copy.25) | copy-start | bytes 12582916
  97.3 4.0 %slice-start.1 = ((s8[8388608]{0:T(1024)(128)(4,1)}), s8[4194304]{0:T(1024)(128)(4,1)S(1)}, s32[]{:S(2)}) async-start(s8[8388608]{0:T(1024)(128)(4,1)} %bitcast.50), calls=%async_computation.6 | async-start | bytes 8388608
  162.3 11.8 %copy-start.1 = (bf16[64,96,2,128]{3,2,1,0:T(2,128)(2,1)S(1)}, bf16[64,96,2,128]{3,2,1,0:T(2,128)(2,1)}, u32[]{:S(2)}) copy-start(bf16[64,96,2,128]{3,2,1,0:T(2,128)(2,1)} %param.13) | copy-start | bytes 9437188
Sparse Core Ops, SparseCore 0:
  17.9 24.3 reduce-scatter.2
  45.1 37.9 all-gather.2
  104.8 57.4 reduce-scatter.4

commit v2 on v1

v2 whole, which is shorter than its diff:
```python
import functools
import jax
import jax.numpy as jnp
from jax import lax
from jax.experimental import pallas as pl
from jax.experimental.pallas import tpu as pltpu
from jax.sharding import PartitionSpec as P

MESH = pl.DeviceIdType.MESH
VMEM_BYTES = 56 * 1024 * 1024


def attend(queries, cached_keys, cached_values, lengths):
    row_count, head_count, head_depth = queries.shape
    kv_count = cached_keys.shape[2]
    group_size = head_count // kv_count
    query_rows = queries.reshape(row_count, kv_count, group_size, head_depth)
    scores = jnp.einsum(
        "rkgd,rckd->rkgc", query_rows, cached_keys, preferred_element_type=jnp.float32
    ) * head_depth ** (-0.5)
    live_mask = jnp.arange(cached_keys.shape[1], dtype=jnp.int32)[None, :] < lengths[:, None]
    scores = jnp.where(live_mask[:, None, None, :], scores, -1e30)
    attn_probs = jax.nn.softmax(scores, axis=-1).astype(jnp.bfloat16)
    context = jnp.einsum(
        "rkgc,rckd->rkgd", attn_probs, cached_values, preferred_element_type=jnp.float32
    )
    return context.reshape(row_count, head_count * head_depth).astype(jnp.bfloat16)


def greet(n_ep, n_x, ep, x, core):
    barrier = pltpu.get_barrier_semaphore()
    for d in range(1, n_ep):
        pl.semaphore_signal(barrier, inc=1, device_id={"ep": lax.rem(ep + d, n_ep)}, device_id_type=MESH)
    for d in range(1, n_x):
        peer = lax.rem(x + d, n_x) * 2 + core
        pl.semaphore_signal(barrier, inc=1, device_id={"tp": peer}, device_id_type=MESH)
    for d in range(n_x):
        peer = lax.rem(x + d, n_x) * 2 + 1 - core
        pl.semaphore_signal(barrier, inc=1, device_id={"tp": peer}, device_id_type=MESH)
    pl.semaphore_wait(barrier, n_ep - 1 + 2 * n_x - 1)


def remote(src, dst, send_sem, recv_sem, where):
    return pltpu.make_async_remote_copy(
        src_ref=src, dst_ref=dst, send_sem=send_sem, recv_sem=recv_sem, device_id=where, device_id_type=MESH
    )


def gather_kernel(
    n_ep, n_tp, partial_ref, gain_ref, out_ref, outgoing, incoming,
    tp_send, tp_recv, ep_send, ep_recv, x_send, x_recv, sib_send, sib_recv,
):
    n_x = n_tp // 2
    ep = lax.axis_index("ep")
    tp = lax.axis_index("tp")
    x, core = tp // 2, lax.rem(tp, 2)
    outgoing[...] = partial_ref[...].astype(jnp.bfloat16)
    greet(n_ep, n_x, ep, x, core)
    started = []
    for d in range(1, n_tp):
        to = lax.rem(tp + d, n_tp)
        piece = lax.rem(to, 2) * n_x + to // 2
        copy = remote(outgoing.at[piece], incoming.at[d], tp_send.at[d], tp_recv.at[d], {"tp": to})
        copy.start()
        started.append(copy)
    total = partial_ref[core * n_x + x]
    for d in range(1, n_tp):
        started[d - 1].wait_recv()
        total += incoming[d].astype(jnp.float32)
    scale = lax.rsqrt(jnp.mean(total * total, axis=-1, keepdims=True) + 1e-06)
    out_ref[ep, core, x] = (total * scale * gain_ref[...]).astype(jnp.bfloat16)

    arriving = []
    for d in range(1, n_ep):
        mine = out_ref.at[ep, core, x]
        copy = remote(mine, mine, ep_send.at[d], ep_recv.at[d], {"ep": lax.rem(ep + d, n_ep)})
        copy.start()
        started.append(copy)
        arriving.append(copy)
    crossing, sibling = {}, []
    for d in range(n_ep + 1):
        if d < n_ep:
            if d > 0:
                arriving[d - 1].wait_recv()
            block = lax.rem(ep - d + n_ep, n_ep)
            part = out_ref.at[block, core, x]
            for k in range(1, n_x):
                to = lax.rem(x + k, n_x) * 2 + core
                copy = remote(part, part, x_send.at[d, k], x_recv.at[d, k], {"tp": to})
                copy.start()
                started.append(copy)
                crossing[d, k] = copy
            copy = remote(part, part, sib_send.at[d, 0], sib_recv.at[d, 0], {"tp": x * 2 + 1 - core})
            copy.start()
            started.append(copy)
            sibling.append(copy)
        if d > 0:
            block = lax.rem(ep - (d - 1) + n_ep, n_ep)
            for k in range(1, n_x):
                crossing[d - 1, k].wait_recv()
                part = out_ref.at[block, core, lax.rem(x - k + n_x, n_x)]
                copy = remote(part, part, sib_send.at[d - 1, k], sib_recv.at[d - 1, k], {"tp": x * 2 + 1 - core})
                copy.start()
                started.append(copy)
                sibling.append(copy)
    for copy in sibling:
        copy.wait_recv()
    for copy in started:
        copy.wait_send()


def gather_latent(partial, gain, n_ep, n_tp):
    rows, width = partial.shape
    part = rows // n_tp
    n_x = n_tp // 2
    dma = pltpu.SemaphoreType.DMA
    out = pl.pallas_call(
        functools.partial(gather_kernel, n_ep, n_tp),
        out_shape=jax.ShapeDtypeStruct((n_ep, 2, n_x, part, width), jnp.bfloat16),
        in_specs=[pl.BlockSpec(memory_space=pltpu.VMEM)] * 2,
        out_specs=pl.BlockSpec(memory_space=pltpu.VMEM),
        scratch_shapes=[
            pltpu.VMEM((n_tp, part, width), jnp.bfloat16),
            pltpu.VMEM((n_tp, part, width), jnp.bfloat16),
            dma((n_tp,)), dma((n_tp,)), dma((n_ep,)), dma((n_ep,)),
            dma((n_ep, n_x)), dma((n_ep, n_x)), dma((n_ep, n_x)), dma((n_ep, n_x)),
        ],
        compiler_params=pltpu.CompilerParams(
            collective_id=0, has_side_effects=True, vmem_limit_bytes=VMEM_BYTES
        ),
        name="gather_latent",
    )(partial.reshape(n_tp, part, width), gain.reshape(1, width))
    return out.reshape(n_ep * rows, width)


def reduce_kernel(
    n_ep, n_tp, mix_ref, out_ref, from_sib, to_x, from_x, to_ep, from_ep,
    sib_send, sib_recv, x_send, x_recv, ep_send, ep_recv, g_send, g_recv,
):
    n_x = n_tp // 2
    ep = lax.axis_index("ep")
    tp = lax.axis_index("tp")
    x, core = tp // 2, lax.rem(tp, 2)
    other = {"tp": x * 2 + 1 - core}
    order = list(range(1, n_ep)) + [0]
    started = []
    greet(n_ep, n_x, ep, x, core)
    sib = {}
    for d in order:
        block = lax.rem(ep + d, n_ep)
        copy = remote(mix_ref.at[block, 1 - core], from_sib.at[d], sib_send.at[d], sib_recv.at[d], other)
        copy.start()
        started.append(copy)
        sib[d] = copy
    crossing = {}
    for d in order:
        block = lax.rem(ep + d, n_ep)
        sib[d].wait_recv()
        for k in range(1, n_x):
            to = lax.rem(x + k, n_x)
            to_x[d, k] = (
                mix_ref[block, core, to].astype(jnp.float32) + from_sib[d, to].astype(jnp.float32)
            ).astype(jnp.bfloat16)
            copy = remote(
                to_x.at[d, k], from_x.at[d, k], x_send.at[d, k], x_recv.at[d, k], {"tp": to * 2 + core}
            )
            copy.start()
            started.append(copy)
            crossing[d, k] = copy
    arriving = []
    for d in order:
        block = lax.rem(ep + d, n_ep)
        total = mix_ref[block, core, x].astype(jnp.float32) + from_sib[d, x].astype(jnp.float32)
        for k in range(1, n_x):
            crossing[d, k].wait_recv()
            total += from_x[d, k].astype(jnp.float32)
        if d > 0:
            to_ep[d] = total.astype(jnp.bfloat16)
            copy = remote(to_ep.at[d], from_ep.at[d], ep_send.at[d], ep_recv.at[d], {"ep": block})
            copy.start()
            started.append(copy)
            arriving.append(copy)
    for d in range(1, n_ep):
        arriving[d - 1].wait_recv()
        total += from_ep[d].astype(jnp.float32)
    out_ref[core, x] = total.astype(jnp.bfloat16)

    part = out_ref.at[core, x]
    last, sibling = [], []
    for k in range(1, n_x):
        to = lax.rem(x + k, n_x) * 2 + core
        copy = remote(part, part, g_send.at[0, k], g_recv.at[0, k], {"tp": to})
        copy.start()
        started.append(copy)
        last.append(copy)
    copy = remote(part, part, g_send.at[1, 0], g_recv.at[1, 0], other)
    copy.start()
    started.append(copy)
    sibling.append(copy)
    for k in range(1, n_x):
        last[k - 1].wait_recv()
        moved = out_ref.at[core, lax.rem(x - k + n_x, n_x)]
        copy = remote(moved, moved, g_send.at[1, k], g_recv.at[1, k], other)
        copy.start()
        started.append(copy)
        sibling.append(copy)
    for copy in sibling:
        copy.wait_recv()
    for copy in started:
        copy.wait_send()


def reduce_mixture(mixture, n_ep, n_tp):
    n_x = n_tp // 2
    part, width = mixture.shape[-2:]
    dma = pltpu.SemaphoreType.DMA
    out = pl.pallas_call(
        functools.partial(reduce_kernel, n_ep, n_tp),
        out_shape=jax.ShapeDtypeStruct((2, n_x, part, width), jnp.bfloat16),
        in_specs=[pl.BlockSpec(memory_space=pltpu.VMEM)],
        out_specs=pl.BlockSpec(memory_space=pltpu.VMEM),
        scratch_shapes=[
            pltpu.VMEM((n_ep, n_x, part, width), jnp.bfloat16),
            pltpu.VMEM((n_ep, n_x, part, width), jnp.bfloat16),
            pltpu.VMEM((n_ep, n_x, part, width), jnp.bfloat16),
            pltpu.VMEM((n_ep, part, width), jnp.bfloat16),
            pltpu.VMEM((n_ep, part, width), jnp.bfloat16),
            dma((n_ep,)), dma((n_ep,)), dma((n_ep, n_x)), dma((n_ep, n_x)),
            dma((n_ep,)), dma((n_ep,)), dma((2, n_x)), dma((2, n_x)),
        ],
        compiler_params=pltpu.CompilerParams(
            collective_id=1, has_side_effects=True, vmem_limit_bytes=VMEM_BYTES
        ),
        name="reduce_mixture",
    )(mixture)
    return out.reshape(n_tp * part, width)


def expert_kernel(step_count, chunk, latent_ref, ids_ref, router_ref, gate_up_ref, down_ref, out_ref, total, gates):
    step = pl.program_id(0)
    depth = latent_ref.shape[1]

    @pl.when(step == 0)
    def _():
        logits = jnp.dot(latent_ref[...], router_ref[...], preferred_element_type=jnp.float32)
        lane = lax.broadcasted_iota(jnp.int32, logits.shape, 1)
        chosen = jnp.zeros(logits.shape, jnp.float32)
        for k in range(ids_ref.shape[1]):
            chosen += (ids_ref[:, k : k + 1] == lane).astype(jnp.float32)
        weighted = chosen * jax.nn.sigmoid(logits)
        gates[...] = weighted / jnp.sum(weighted, axis=-1, keepdims=True)

    which = lax.axis_index("ep") * step_count + step
    lane = lax.broadcasted_iota(jnp.int32, gates.shape, 1)
    own = jnp.sum(jnp.where(lane == which, gates[...], 0.0), axis=1, keepdims=True)
    gate_part, up_part = None, None
    for k in range(0, depth, chunk):
        rows = latent_ref[:, k : k + chunk]
        gate_step = jnp.dot(rows, gate_up_ref[0, k : k + chunk, 0, :], preferred_element_type=jnp.float32)
        up_step = jnp.dot(rows, gate_up_ref[0, k : k + chunk, 1, :], preferred_element_type=jnp.float32)
        gate_part = gate_step if gate_part is None else gate_part + gate_step
        up_part = up_step if up_part is None else up_part + up_step
    hidden = (jax.nn.silu(gate_part) * up_part * own).astype(jnp.bfloat16)
    out_step = jnp.dot(hidden, down_ref[0], preferred_element_type=jnp.float32)

    @pl.when(step == 0)
    def _():
        total[...] = out_step

    @pl.when(step > 0)
    def _():
        total[...] += out_step

    @pl.when(step == step_count - 1)
    def _():
        out_ref[...] = total[...].astype(jnp.bfloat16)


def run_experts(latent, ids, router, w_gate_up, w_down):
    local_count, width, _, hidden_dev = w_gate_up.shape
    rows = latent.shape[0]
    expert_total = router.shape[1]
    return pl.pallas_call(
        functools.partial(expert_kernel, local_count, 512),
        grid=(local_count,),
        out_shape=jax.ShapeDtypeStruct((rows, width), jnp.bfloat16),
        in_specs=[
            pl.BlockSpec((rows, width), lambda i: (0, 0)),
            pl.BlockSpec(ids.shape, lambda i: (0, 0)),
            pl.BlockSpec(router.shape, lambda i: (0, 0)),
            pl.BlockSpec((1, width, 2, hidden_dev), lambda i: (i, 0, 0, 0)),
            pl.BlockSpec((1, hidden_dev, width), lambda i: (i, 0, 0)),
        ],
        out_specs=pl.BlockSpec((rows, width), lambda i: (0, 0)),
        scratch_shapes=[
            pltpu.VMEM((rows, width), jnp.float32),
            pltpu.VMEM((rows, expert_total), jnp.float32),
        ],
        compiler_params=pltpu.CompilerParams(vmem_limit_bytes=VMEM_BYTES),
        name="run_experts",
    )(latent, ids, router, w_gate_up, w_down)


def body(
    n_ep, n_tp, queries, cached_keys, cached_values, lengths, expert_ids,
    latent_proj, latent_gain, router, w_gate_up, w_down, w_up,
):
    rows = expert_ids.shape[0]
    all_ids = lax.all_gather(expert_ids, "ep", axis=0, tiled=True)
    context = attend(queries, cached_keys, cached_values, lengths)
    partial_value = jnp.dot(context, latent_proj, preferred_element_type=jnp.float32)
    latent = gather_latent(partial_value, latent_gain, n_ep, n_tp)
    mixture = run_experts(latent, all_ids, router, w_gate_up, w_down)
    part = rows // n_tp
    mixture = mixture.reshape(n_ep, 2, n_tp // 2, part, mixture.shape[-1])
    combined = reduce_mixture(mixture, n_ep, n_tp)
    return jnp.dot(combined, w_up, preferred_element_type=jnp.float32).astype(jnp.bfloat16)


def solution(mesh):
    return jax.shard_map(
        functools.partial(body, mesh.shape["ep"], mesh.shape["tp"]),
        mesh=mesh,
        in_specs=(
            P(("groups", "ep"), "tp", None),
            P(("groups", "ep"), None, "tp", None),
            P(("groups", "ep"), None, "tp", None),
            P(("groups", "ep")),
            P(("groups", "ep"), None),
            P("tp", None),
            P(),
            P(),
            P("ep", None, None, "tp"),
            P("ep", "tp", None),
            P(None, "tp"),
        ),
        out_specs=P(("groups", "ep"), "tp"),
        check_vma=False,
    )
```

time: 181 us -> 121 us (0.67)
  Pallas kernels: 0 us -> 87.3 us
  waiting for transfers between devices: 82.1 us -> 0 us
  local copies, waits for them, and re-layouts: 32.8 us -> 1.84 us
  between operations: 13.3 us -> 0.06 us
  matrix products: 28.6 us -> 16.1 us
  blocking collectives: 19.5 us -> 15.1 us
  other arithmetic: 4.2 us -> 0.88 us
    pallas_call x0 -> x3, Pallas kernels: none -> 87.3 us  [the longest x1 44.5 us: run_experts(): pl.pallas_call(functools.partial(expert_kernel, local_count, 512), grid=(...]
    reduce_scatter x2 -> x0, waiting for transfers between devices: 82 us -> none  [the longest x1 57.6 us: body(): lax.psum_scatter(mixture, ('ep', 'tp'), scatter_dimension=0, tiled=True)]
    slice x2 -> x0, local copies, waits for them, and re-layouts: 16 us -> none  [the longest x1 16 us: body(): gate_up = jnp.dot(latent, paired[e], preferred_element_type=jnp.float32)]
    unnamed x31 -> x5, local copies, waits for them, and re-layouts: 16.7 us -> 1.02 us
    dot_general x6 -> x0, matrix products: 12.7 us -> none  [the longest x4 7.64 us: body(): gate_up = jnp.dot(latent, paired[e], preferred_element_type=jnp.float32)]
    all_gather x1 -> x0, blocking collectives: 6.12 us -> none  [body(): combined = lax.all_gather(part, 'tp', axis=0, tiled=True)]
    convert_element_type x3 -> x0, other arithmetic: 2.25 us -> none  [the longest x1 1.62 us: body(): latent = (summed * lax.rsqrt(jnp.mean(summed * summed, axis=-1, keepdims=...]
  transfers between devices with their start and end apart: 3 -> 0, of which waited for: 2 -> 0; matrix products, arithmetic and copies ran while one was open for 17% -> 0% of each run, Pallas kernels for 0% -> 0%
where the time goes in v2:
time: 121 us
  Pallas kernels  87.3 us (72%)
  matrix products  16.1 us (13%)
  blocking collectives  15.1 us (12%)
  local copies, waits for them, and re-layouts  1.84 us (2%)
    pallas_call x1, Pallas kernels, run_experts(): pl.pallas_call(functools.partial(expert_kernel, local_count, 512), grid=(...  44.5 us
    pallas_call x1, Pallas kernels, gather_latent(): pl.pallas_call(functools.partial(gather_kernel, n_ep, n_tp), out_shape=ja...  21.4 us
    pallas_call x1, Pallas kernels, reduce_mixture(): pl.pallas_call(functools.partial(reduce_kernel, n_ep, n_tp), out_shape=ja...  21.3 us
    all_gather x1, blocking collectives, body(): all_ids = lax.all_gather(expert_ids, 'ep', axis=0, tiled=True)  15.1 us
    dot_general x1, matrix products, body(): jnp.dot(combined, w_up, preferred_element_type=jnp.float32)  5.76 us
    sub x1, matrix products, attend(): attn_probs = jax.nn.softmax(scores, axis=-1).astype(jnp.bfloat16)  4.53 us
    dot_general x1, matrix products, body(): jnp.dot(context, latent_proj, preferred_element_type=jnp.float32)  3.88 us

profile of v2, /device:TPU:0, one launch (start us, length us, event | category | flops | bytes accessed | tf_op | source)
XLA Modules:
  0.0 121.2 jit_solution(9738029605412058534)
XLA Ops:
  0.0 0.0 copy-start
  0.0 0.9 iota_compare_fusion
  0.9 15.1 %all-gather = s32[4,64,8]{1,2,0:T(8,128)S(1)} all-gather(s32[1,64,8]{1,2,0:T(8,128)} %bitcast.19), channel_id=1, replica_groups=mesh['groups'=2,'ep'=4,'tp'=4] {'ep'}, dimensions={0}, use_global_device_ids=true | all-gather | bytes 10240 | tf_op jit(solution)/shard_map/all_gather | solution.py:309
  16.0 0.7 copy.18
  16.7 4.5 %fusion.19 = (f32[64,2,4]{2,1,0:T(2,128)S(1)}, f32[64,2,4,96]{3,2,1,0:T(4,128)}) fusion(bf16[64,2,4,128]{3,2,1,0:T(4,128)(2,1)} %bitcast.20, bf16[64,96,2,128]{3,2,1,0:T(2,128)(2,1)} %param.12, pred[64,96]{1,0:T(8,128)(4,1)S(1)} %iota_compare_fusion), kind=kOutput, calls=%fused_computation.16 | convolution fusion | flops 12779615 | bytes 3481600 | tf_op jit(solution)/shard_map/sub | solution.py:23
  21.2 0.0 copy-done
  21.2 1.9 %fusion.15 = bf16[64,2,4,128]{3,2,1,0:T(4,128)(2,1)S(1)} fusion(bf16[64,96,2,128]{3,2,1,0:T(2,128)(2,1)S(1)} %copy-done, f32[64,2,4,96]{3,2,1,0:T(4,128)} %get-tuple-element.6, f32[64,2,4]{2,1,0:T(2,128)S(1)} %get-tuple-element.5), kind=kOutput, calls=%fused_computation.12 | convolution fusion | flops 12746752 | bytes 3475456 | tf_op jit(solution)/shard_map/rkgc,rckd->rkgd/dot_general | solution.py:24
  23.2 0.1 convert_element_type.15
  23.3 0.0 copy-start.1
  23.3 3.9 %fusion.1.partial_ref = f32[4,16,2048]{2,1,0:T(8,128)} fusion(bf16[4,16,1024]{2,1,0:T(8,128)(2,1)S(1)} %convert_element_type.15, bf16[1024,2048]{1,0:T(8,128)(2,1)} %param.16), kind=kOutput, calls=%fused_computation.1 | convolution fusion | flops 268435456 | bytes 4849664 | tf_op jit(solution)/shard_map/dot_general | solution.py:311
  27.2 21.4 %gather_latent.1 = bf16[4,2,2,16,2048]{4,3,2,1,0:T(8,128)(2,1)} custom-call(f32[4,16,2048]{2,1,0:T(8,128)} %fusion.1.partial_ref, f32[1,2048]{1,0:T(1,128)} %bitcast.18), custom_call_target="tpu_custom_call" | custom-call | tf_op jit(solution)/shard_map/gather_latent/pallas_call | solution.py:117
  48.6 0.0 copy-done.1
  48.6 1.0 copy.19.router_ref
  49.6 44.5 %run_experts.1 = bf16[256,2048]{1,0:T(8,128)(2,1)} custom-call(bf16[256,2048]{1,0:T(8,128)(2,1)} %bitcast.15, s32[256,8]{1,0:T(8,128)} %bitcast.17, bf16[2048,16]{1,0:T(8,128)(2,1)} %copy.19.router_ref, bf16[4,2048,2,512]{3,2,1,0:T(2,128)(2,1)} %gate_up_ref.1, bf16[4,512,2048]{2,1,0:T(8,128)(2,1)} %down_ref.1), custom_call_target="tpu_custom_call" | custom-call | tf_op jit(solution)/shard_map/run_experts/pallas_call | solution.py:283
  94.2 21.3 %reduce_mixture.1 = bf16[2,2,16,2048]{3,2,1,0:T(8,128)(2,1)} custom-call(bf16[4,2,2,16,2048]{4,3,2,1,0:T(8,128)(2,1)} %bitcast.14), custom_call_target="tpu_custom_call" | custom-call | tf_op jit(solution)/shard_map/reduce_mixture/pallas_call | solution.py:217
  115.5 5.8 %convolution_convert_fusion = bf16[64,2048]{1,0:T(8,128)(2,1)} fusion(bf16[64,2048]{1,0:T(8,128)(2,1)} %bitcast.16, bf16[2048,2048]{1,0:T(8,128)(2,1)} %param.21), kind=kOutput, calls=%fused_computation.7 | convolution fusion | flops 537001984 | bytes 8912896 | tf_op jit(solution)/shard_map/dot_general | solution.py:317
Async XLA Ops:
  0.0 21.2 %copy-start = (bf16[64,96,2,128]{3,2,1,0:T(2,128)(2,1)S(1)}, bf16[64,96,2,128]{3,2,1,0:T(2,128)(2,1)}, u32[]{:S(2)}) copy-start(bf16[64,96,2,128]{3,2,1,0:T(2,128)(2,1)} %param.13) | copy-start | bytes 9437188
  23.3 25.3 %copy-start.1 = (bf16[2048,16]{0,1:T(8,128)(2,1)S(1)}, bf16[2048,16]{0,1:T(8,128)(2,1)}, u32[]{:S(2)}) copy-start(bf16[2048,16]{0,1:T(8,128)(2,1)} %param.18) | copy-start | bytes 196612

commit v3 on v2

--- a/solution.py
+++ b/solution.py
@@ -47,8 +47,8 @@
 
 
 def gather_kernel(
-    n_ep, n_tp, partial_ref, gain_ref, out_ref, outgoing, incoming,
-    tp_send, tp_recv, ep_send, ep_recv, x_send, x_recv, sib_send, sib_recv,
+    n_ep, n_tp, partial_ref, gain_ref, ids_ref, out_ref, all_ids_ref, outgoing, incoming,
+    tp_send, tp_recv, ep_send, ep_recv, x_send, x_recv, sib_send, sib_recv, ids_send, ids_recv,
 ):
     n_x = n_tp // 2
     ep = lax.axis_index("ep")
@@ -63,6 +63,15 @@
         copy = remote(outgoing.at[piece], incoming.at[d], tp_send.at[d], tp_recv.at[d], {"tp": to})
         copy.start()
         started.append(copy)
+    all_ids_ref[ep] = ids_ref[...]
+    labels = []
+    for d in range(1, n_ep):
+        copy = remote(
+            ids_ref, all_ids_ref.at[ep], ids_send.at[d], ids_recv.at[d], {"ep": lax.rem(ep + d, n_ep)}
+        )
+        copy.start()
+        started.append(copy)
+        labels.append(copy)
     total = partial_ref[core * n_x + x]
     for d in range(1, n_tp):
         started[d - 1].wait_recv()
@@ -105,32 +114,37 @@
                 sibling.append(copy)
     for copy in sibling:
         copy.wait_recv()
+    for copy in labels:
+        copy.wait_recv()
     for copy in started:
         copy.wait_send()
 
 
-def gather_latent(partial, gain, n_ep, n_tp):
+def gather_latent(partial, gain, ids, n_ep, n_tp):
     rows, width = partial.shape
     part = rows // n_tp
     n_x = n_tp // 2
     dma = pltpu.SemaphoreType.DMA
-    out = pl.pallas_call(
+    out, all_ids = pl.pallas_call(
         functools.partial(gather_kernel, n_ep, n_tp),
-        out_shape=jax.ShapeDtypeStruct((n_ep, 2, n_x, part, width), jnp.bfloat16),
-        in_specs=[pl.BlockSpec(memory_space=pltpu.VMEM)] * 2,
-        out_specs=pl.BlockSpec(memory_space=pltpu.VMEM),
+        out_shape=(
+            jax.ShapeDtypeStruct((n_ep, 2, n_x, part, width), jnp.bfloat16),
+            jax.ShapeDtypeStruct((n_ep,) + ids.shape, ids.dtype),
+        ),
+        in_specs=[pl.BlockSpec(memory_space=pltpu.VMEM)] * 3,
+        out_specs=[pl.BlockSpec(memory_space=pltpu.VMEM)] * 2,
         scratch_shapes=[
             pltpu.VMEM((n_tp, part, width), jnp.bfloat16),
             pltpu.VMEM((n_tp, part, width), jnp.bfloat16),
             dma((n_tp,)), dma((n_tp,)), dma((n_ep,)), dma((n_ep,)),
-            dma((n_ep, n_x)), dma((n_ep, n_x)), dma((n_ep, n_x)), dma((n_ep, n_x)),
+            dma((n_ep, n_x)), dma((n_ep, n_x)), dma((n_ep, n_x)), dma((n_ep, n_x)), dma((n_ep,)), dma((n_ep,)),
         ],
         compiler_params=pltpu.CompilerParams(
             collective_id=0, has_side_effects=True, vmem_limit_bytes=VMEM_BYTES
         ),
         name="gather_latent",
-    )(partial.reshape(n_tp, part, width), gain.reshape(1, width))
-    return out.reshape(n_ep * rows, width)
+    )(partial.reshape(n_tp, part, width), gain.reshape(1, width), ids)
+    return out.reshape(n_ep * rows, width), all_ids.reshape(n_ep * rows, ids.shape[1])
 
 
 def reduce_kernel(
@@ -236,11 +250,15 @@
     return out.reshape(n_tp * part, width)
 
 
-def expert_kernel(step_count, chunk, latent_ref, ids_ref, router_ref, gate_up_ref, down_ref, out_ref, total, gates):
-    step = pl.program_id(0)
-    depth = latent_ref.shape[1]
-
-    @pl.when(step == 0)
+def expert_kernel(
+    latent_ref, ids_ref, router_ref, left_ref, right_ref, down_ref, out_ref, total, gates, spread
+):
+    expert, part = pl.program_id(0), pl.program_id(1)
+    first = (expert == 0) & (part == 0)
+    final = (expert == pl.num_programs(0) - 1) & (part == pl.num_programs(1) - 1)
+    rows, depth = latent_ref.shape
+
+    @pl.when(first)
     def _():
         logits = jnp.dot(latent_ref[...], router_ref[...], preferred_element_type=jnp.float32)
         lane = lax.broadcasted_iota(jnp.int32, logits.shape, 1)
@@ -249,29 +267,28 @@
             chosen += (ids_ref[:, k : k + 1] == lane).astype(jnp.float32)
         weighted = chosen * jax.nn.sigmoid(logits)
         gates[...] = weighted / jnp.sum(weighted, axis=-1, keepdims=True)
-
-    which = lax.axis_index("ep") * step_count + step
+        source = lax.broadcasted_iota(jnp.int32, (256, 512), 0)
+        target = lax.broadcasted_iota(jnp.int32, (256, 512), 1)
+        to_gate = (target == 2 * source).astype(jnp.bfloat16)
+        to_up = (target == 2 * source + 1).astype(jnp.bfloat16)
+        for k in range(0, depth, 256):
+            piece = latent_ref[:, k : k + 256]
+            at = slice(2 * k, 2 * k + 512)
+            spread[:rows, at] = jnp.dot(piece, to_gate, preferred_element_type=jnp.float32).astype(jnp.bfloat16)
+            spread[rows:, at] = jnp.dot(piece, to_up, preferred_element_type=jnp.float32).astype(jnp.bfloat16)
+        total[...] = jnp.zeros_like(total)
+
+    which = lax.axis_index("ep") * pl.num_programs(0) + expert
     lane = lax.broadcasted_iota(jnp.int32, gates.shape, 1)
     own = jnp.sum(jnp.where(lane == which, gates[...], 0.0), axis=1, keepdims=True)
-    gate_part, up_part = None, None
-    for k in range(0, depth, chunk):
-        rows = latent_ref[:, k : k + chunk]
-        gate_step = jnp.dot(rows, gate_up_ref[0, k : k + chunk, 0, :], preferred_element_type=jnp.float32)
-        up_step = jnp.dot(rows, gate_up_ref[0, k : k + chunk, 1, :], preferred_element_type=jnp.float32)
-        gate_part = gate_step if gate_part is None else gate_part + gate_step
-        up_part = up_step if up_part is None else up_part + up_step
-    hidden = (jax.nn.silu(gate_part) * up_part * own).astype(jnp.bfloat16)
-    out_step = jnp.dot(hidden, down_ref[0], preferred_element_type=jnp.float32)
-
-    @pl.when(step == 0)
-    def _():
-        total[...] = out_step
-
-    @pl.when(step > 0)
-    def _():
-        total[...] += out_step
-
-    @pl.when(step == step_count - 1)
+    weights = jnp.concatenate(
+        [left_ref.at[0].reshape(2 * depth, 128)[...], right_ref.at[0].reshape(2 * depth, 128)[...]], axis=1
+    )
+    both = jnp.dot(spread[...], weights, preferred_element_type=jnp.float32)
+    hidden = (jax.nn.silu(both[:rows]) * both[rows:] * own).astype(jnp.bfloat16)
+    total[...] += jnp.dot(hidden, down_ref[0], preferred_element_type=jnp.float32)
+
+    @pl.when(final)
     def _():
         out_ref[...] = total[...].astype(jnp.bfloat16)
 
@@ -281,24 +298,26 @@
     rows = latent.shape[0]
     expert_total = router.shape[1]
     return pl.pallas_call(
-        functools.partial(expert_kernel, local_count, 512),
-        grid=(local_count,),
+        expert_kernel,
+        grid=(local_count, hidden_dev // 256),
         out_shape=jax.ShapeDtypeStruct((rows, width), jnp.bfloat16),
         in_specs=[
-            pl.BlockSpec((rows, width), lambda i: (0, 0)),
-            pl.BlockSpec(ids.shape, lambda i: (0, 0)),
-            pl.BlockSpec(router.shape, lambda i: (0, 0)),
-            pl.BlockSpec((1, width, 2, hidden_dev), lambda i: (i, 0, 0, 0)),
-            pl.BlockSpec((1, hidden_dev, width), lambda i: (i, 0, 0)),
+            pl.BlockSpec((rows, width), lambda i, j: (0, 0)),
+            pl.BlockSpec(ids.shape, lambda i, j: (0, 0)),
+            pl.BlockSpec(router.shape, lambda i, j: (0, 0)),
+            pl.BlockSpec((1, width, 2, 128), lambda i, j: (i, 0, 0, 2 * j)),
+            pl.BlockSpec((1, width, 2, 128), lambda i, j: (i, 0, 0, 2 * j + 1)),
+            pl.BlockSpec((1, 256, width), lambda i, j: (i, j, 0)),
         ],
-        out_specs=pl.BlockSpec((rows, width), lambda i: (0, 0)),
+        out_specs=pl.BlockSpec((rows, width), lambda i, j: (0, 0)),
         scratch_shapes=[
             pltpu.VMEM((rows, width), jnp.float32),
             pltpu.VMEM((rows, expert_total), jnp.float32),
+            pltpu.VMEM((2 * rows, 2 * width), jnp.bfloat16),
         ],
         compiler_params=pltpu.CompilerParams(vmem_limit_bytes=VMEM_BYTES),
         name="run_experts",
-    )(latent, ids, router, w_gate_up, w_down)
+    )(latent, ids, router, w_gate_up, w_gate_up, w_down)
 
 
 def body(
@@ -306,10 +325,9 @@
     latent_proj, latent_gain, router, w_gate_up, w_down, w_up,
 ):
     rows = expert_ids.shape[0]
-    all_ids = lax.all_gather(expert_ids, "ep", axis=0, tiled=True)
     context = attend(queries, cached_keys, cached_values, lengths)
     partial_value = jnp.dot(context, latent_proj, preferred_element_type=jnp.float32)
-    latent = gather_latent(partial_value, latent_gain, n_ep, n_tp)
+    latent, all_ids = gather_latent(partial_value, latent_gain, expert_ids, n_ep, n_tp)
     mixture = run_experts(latent, all_ids, router, w_gate_up, w_down)
     part = rows // n_tp
     mixture = mixture.reshape(n_ep, 2, n_tp // 2, part, mixture.shape[-1])

time: 121 us -> 88.3 us (0.73)
  Pallas kernels: 87.3 us -> 68.5 us
  blocking collectives: 15.1 us -> 0 us
    pallas_call x2, Pallas kernels: 66 us -> 47.4 us  [the longest x1 23.7 us: run_experts(): pl.pallas_call(expert_kernel, grid=(local_count, hidden_dev // 256), out_...]
    all_gather x1 -> x0, blocking collectives: 15.1 us -> none  [body(): all_ids = lax.all_gather(expert_ids, 'ep', axis=0, tiled=True)]
    unnamed x5 -> x6, local copies, waits for them, and re-layouts: 1.02 us -> 2.46 us
where the time goes in v3:
time: 88.3 us; the launch traced here: 88.1 us
  Pallas kernels  68.5 us (78%)
  matrix products  16.1 us (18%)
  local copies, waits for them, and re-layouts  2.53 us (3%)
    pallas_call x1, Pallas kernels, run_experts(): pl.pallas_call(expert_kernel, grid=(local_count, hidden_dev // 256), out_...  23.7 us
    pallas_call x1, Pallas kernels, gather_latent(): pl.pallas_call(functools.partial(gather_kernel, n_ep, n_tp), out_shape=(j...  23.7 us
    pallas_call x1, Pallas kernels, reduce_mixture(): pl.pallas_call(functools.partial(reduce_kernel, n_ep, n_tp), out_shape=ja...  21.1 us
    dot_general x1, matrix products, body(): jnp.dot(combined, w_up, preferred_element_type=jnp.float32)  5.76 us
    sub x1, matrix products, attend(): attn_probs = jax.nn.softmax(scores, axis=-1).astype(jnp.bfloat16)  4.53 us
    dot_general x1, matrix products, body(): jnp.dot(context, latent_proj, preferred_element_type=jnp.float32)  3.85 us
    unnamed x6, local copies, waits for them, and re-layouts  2.46 us
    dot_general x1, matrix products, attend(): jnp.einsum('rkgc,rckd->rkgd', attn_probs, cached_values, preferred_elemen...  1.94 us

profile of v3, /device:TPU:0, one launch (start us, length us, event | category | flops | bytes accessed | tf_op | source)
XLA Modules:
  0.0 88.1 jit_solution(18018789291465630202)
XLA Ops:
  0.0 0.0 copy-start
  0.0 0.9 iota_compare_fusion
  0.9 1.4 %copy.14.ids_ref = s32[64,8]{1,0:T(8,128)} copy(s32[64,8]{0,1:T(8,128)} %param.15) | data formatting | bytes 4096 | tf_op args[4]
  2.3 4.5 %fusion.19 = (f32[64,2,4]{2,1,0:T(2,128)S(1)}, f32[64,2,4,96]{3,2,1,0:T(4,128)}) fusion(bf16[64,2,4,128]{3,2,1,0:T(4,128)(2,1)} %bitcast.18, bf16[64,96,2,128]{3,2,1,0:T(2,128)(2,1)} %param.12, pred[64,96]{1,0:T(8,128)(4,1)S(1)} %iota_compare_fusion), kind=kOutput, calls=%fused_computation.16 | convolution fusion | flops 12779615 | bytes 3481600 | tf_op jit(solution)/shard_map/sub | solution.py:23
  6.9 0.0 copy-done
  6.9 1.9 %fusion.15 = bf16[64,2,4,128]{3,2,1,0:T(4,128)(2,1)S(1)} fusion(bf16[64,96,2,128]{3,2,1,0:T(2,128)(2,1)S(1)} %copy-done, f32[64,2,4,96]{3,2,1,0:T(4,128)} %get-tuple-element.10, f32[64,2,4]{2,1,0:T(2,128)S(1)} %get-tuple-element.9), kind=kOutput, calls=%fused_computation.12 | convolution fusion | flops 12746752 | bytes 3475456 | tf_op jit(solution)/shard_map/rkgc,rckd->rkgd/dot_general | solution.py:24
  8.8 0.0 copy-start.1
  8.8 0.1 convert_element_type.15
  8.9 3.9 %fusion.1.partial_ref = f32[4,16,2048]{2,1,0:T(8,128)} fusion(bf16[4,16,1024]{2,1,0:T(8,128)(2,1)S(1)} %convert_element_type.15, bf16[1024,2048]{1,0:T(8,128)(2,1)} %param.16), kind=kOutput, calls=%fused_computation.1 | convolution fusion | flops 268435456 | bytes 4849664 | tf_op jit(solution)/shard_map/dot_general | solution.py:329
  12.8 0.0 copy-done.1
  12.8 1.0 %copy.15.router_ref = bf16[2048,16]{1,0:T(8,128)(2,1)} copy(bf16[2048,16]{0,1:T(8,128)(2,1)S(1)} %copy-done.1) | data formatting | bytes 131072 | tf_op args[7]
  13.8 23.7 %gather_latent.1 = (bf16[4,2,2,16,2048]{4,3,2,1,0:T(8,128)(2,1)}, s32[4,64,8]{2,1,0:T(8,128)}) custom-call(f32[4,16,2048]{2,1,0:T(8,128)} %fusion.1.partial_ref, f32[1,2048]{1,0:T(1,128)} %bitcast.17, s32[64,8]{1,0:T(8,128)} %copy.14.ids_ref), custom_call_target="tpu_custom_call" | custom-call | tf_op jit(solution)/shard_map/gather_latent/pallas_call | solution.py:128
  37.5 23.7 %run_experts.1 = bf16[256,2048]{1,0:T(8,128)(2,1)} custom-call(bf16[256,2048]{1,0:T(8,128)(2,1)} %bitcast.15, s32[256,8]{1,0:T(8,128)} %bitcast.16, bf16[2048,16]{1,0:T(8,128)(2,1)} %copy.15.router_ref, bf16[4,2048,2,512]{3,2,1,0:T(2,128)(2,1)} %right_ref.1, bf16[4,2048,2,512]{3,2,1,0:T(2,128)(2,1)} %right_ref.1, bf16[4,512,2048]{2,1,0:T(8,128)(2,1)} %down_ref.1), custom_call_target="tpu_custom_call" | custom-call | tf_op jit(solution)/shard_map/run_experts/pallas_call | solution.py:300
  61.2 21.1 %reduce_mixture.1 = bf16[2,2,16,2048]{3,2,1,0:T(8,128)(2,1)} custom-call(bf16[4,2,2,16,2048]{4,3,2,1,0:T(8,128)(2,1)} %bitcast.13), custom_call_target="tpu_custom_call" | custom-call | tf_op jit(solution)/shard_map/reduce_mixture/pallas_call | solution.py:231
  82.3 5.8 %convolution_convert_fusion = bf16[64,2048]{1,0:T(8,128)(2,1)} fusion(bf16[64,2048]{1,0:T(8,128)(2,1)} %bitcast.14, bf16[2048,2048]{1,0:T(8,128)(2,1)} %param.21), kind=kOutput, calls=%fused_computation.7 | convolution fusion | flops 537001984 | bytes 8912896 | tf_op jit(solution)/shard_map/dot_general | solution.py:335
Async XLA Ops:
  0.0 6.9 %copy-start = (bf16[64,96,2,128]{3,2,1,0:T(2,128)(2,1)S(1)}, bf16[64,96,2,128]{3,2,1,0:T(2,128)(2,1)}, u32[]{:S(2)}) copy-start(bf16[64,96,2,128]{3,2,1,0:T(2,128)(2,1)} %param.13) | copy-start | bytes 9437188
  8.8 3.9 %copy-start.1 = (bf16[2048,16]{0,1:T(8,128)(2,1)S(1)}, bf16[2048,16]{0,1:T(8,128)(2,1)}, u32[]{:S(2)}) copy-start(bf16[2048,16]{0,1:T(8,128)(2,1)} %param.18) | copy-start | bytes 196612

commit v4 on v3

--- a/solution.py
+++ b/solution.py
@@ -7,7 +7,7 @@
 from jax.sharding import PartitionSpec as P
 
 MESH = pl.DeviceIdType.MESH
-VMEM_BYTES = 56 * 1024 * 1024
+MIB = 1024 * 1024
 
 
 def attend(queries, cached_keys, cached_values, lengths):
@@ -140,7 +140,7 @@
             dma((n_ep, n_x)), dma((n_ep, n_x)), dma((n_ep, n_x)), dma((n_ep, n_x)), dma((n_ep,)), dma((n_ep,)),
         ],
         compiler_params=pltpu.CompilerParams(
-            collective_id=0, has_side_effects=True, vmem_limit_bytes=VMEM_BYTES
+            collective_id=0, has_side_effects=True, vmem_limit_bytes=16 * MIB
         ),
         name="gather_latent",
     )(partial.reshape(n_tp, part, width), gain.reshape(1, width), ids)
@@ -243,7 +243,7 @@
             dma((n_ep,)), dma((n_ep,)), dma((2, n_x)), dma((2, n_x)),
         ],
         compiler_params=pltpu.CompilerParams(
-            collective_id=1, has_side_effects=True, vmem_limit_bytes=VMEM_BYTES
+            collective_id=1, has_side_effects=True, vmem_limit_bytes=16 * MIB
         ),
         name="reduce_mixture",
     )(mixture)
@@ -315,7 +315,7 @@
             pltpu.VMEM((rows, expert_total), jnp.float32),
             pltpu.VMEM((2 * rows, 2 * width), jnp.bfloat16),
         ],
-        compiler_params=pltpu.CompilerParams(vmem_limit_bytes=VMEM_BYTES),
+        compiler_params=pltpu.CompilerParams(vmem_limit_bytes=min(56, 16 + rows // 16) * MIB),
         name="run_experts",
     )(latent, ids, router, w_gate_up, w_gate_up, w_down)
 

time: 88.3 us -> 86.9 us (0.984)
  Pallas kernels: 68.5 us -> 62.3 us
  local copies, waits for them, and re-layouts: 2.53 us -> 7.4 us
    unnamed x6 -> x14, local copies, waits for them, and re-layouts: 2.46 us -> 7.32 us
    pallas_call x1, Pallas kernels: 23.7 us -> 21.4 us  [run_experts(): pl.pallas_call(expert_kernel, grid=(local_count, hidden_dev // 256), out_...]
    pallas_call x1, Pallas kernels: 23.7 us -> 21.6 us  [gather_latent(): pl.pallas_call(functools.partial(gather_kernel, n_ep, n_tp), out_shape=(j...]
    pallas_call x1, Pallas kernels: 21.1 us -> 19.3 us  [reduce_mixture(): pl.pallas_call(functools.partial(reduce_kernel, n_ep, n_tp), out_shape=ja...]
where the time goes in v4:
time: 86.9 us; the launch traced here: 86.6 us
  Pallas kernels  62.3 us (72%)
  matrix products  16 us (18%)
  local copies, waits for them, and re-layouts  7.4 us (9%)
  other arithmetic  0.88 us (1%)
    pallas_call x1, Pallas kernels, gather_latent(): pl.pallas_call(functools.partial(gather_kernel, n_ep, n_tp), out_shape=(j...  21.6 us
    pallas_call x1, Pallas kernels, run_experts(): pl.pallas_call(expert_kernel, grid=(local_count, hidden_dev // 256), out_...  21.4 us
    pallas_call x1, Pallas kernels, reduce_mixture(): pl.pallas_call(functools.partial(reduce_kernel, n_ep, n_tp), out_shape=ja...  19.3 us
    unnamed x14, local copies, waits for them, and re-layouts  7.32 us
    dot_general x1, matrix products, body(): jnp.dot(combined, w_up, preferred_element_type=jnp.float32)  5.67 us
    sub x1, matrix products, attend(): attn_probs = jax.nn.softmax(scores, axis=-1).astype(jnp.bfloat16)  4.53 us
    dot_general x1, matrix products, body(): jnp.dot(context, latent_proj, preferred_element_type=jnp.float32)  3.83 us
    dot_general x1, matrix products, attend(): jnp.einsum('rkgc,rckd->rkgd', attn_probs, cached_values, preferred_elemen...  1.94 us

profile of v4, /device:TPU:0, one launch (start us, length us, event | category | flops | bytes accessed | tf_op | source)
XLA Modules:
  0.0 86.6 jit_solution(6349080531282532138)
XLA Ops:
  0.0 0.0 copy-start
  0.0 0.9 %iota_compare_fusion = pred[64,96]{1,0:T(8,128)(4,1)S(1)} fusion(s32[64]{0:T(128)} %param.14), kind=kLoop, calls=%fused_computation.15 | loop fusion | flops 6144 | bytes 6400 | tf_op jit(solution)/shard_map/lt | solution.py:21
  0.9 0.8 copy.14.ids_ref
  1.7 4.5 %fusion.19 = (f32[64,2,4]{2,1,0:T(2,128)S(1)}, f32[64,2,4,96]{3,2,1,0:T(4,128)}) fusion(bf16[64,2,4,128]{3,2,1,0:T(4,128)(2,1)} %bitcast.18, bf16[64,96,2,128]{3,2,1,0:T(2,128)(2,1)} %param.12, pred[64,96]{1,0:T(8,128)(4,1)S(1)} %iota_compare_fusion), kind=kOutput, calls=%fused_computation.16 | convolution fusion | flops 12779615 | bytes 3481600 | tf_op jit(solution)/shard_map/sub | solution.py:23
  6.3 0.0 copy-done
  6.3 1.9 %fusion.15 = bf16[64,2,4,128]{3,2,1,0:T(4,128)(2,1)S(1)} fusion(bf16[64,96,2,128]{3,2,1,0:T(2,128)(2,1)S(1)} %copy-done, f32[64,2,4,96]{3,2,1,0:T(4,128)} %get-tuple-element.10, f32[64,2,4]{2,1,0:T(2,128)S(1)} %get-tuple-element.9), kind=kOutput, calls=%fused_computation.12 | convolution fusion | flops 12746752 | bytes 3475456 | tf_op jit(solution)/shard_map/rkgc,rckd->rkgd/dot_general | solution.py:24
  8.2 0.0 copy-start.5
  8.2 0.1 convert_element_type.15
  8.3 0.0 copy-start.4
  8.3 3.8 %fusion.1.partial_ref = f32[4,16,2048]{2,1,0:T(8,128)} fusion(bf16[4,16,1024]{2,1,0:T(8,128)(2,1)S(1)} %convert_element_type.15, bf16[1024,2048]{1,0:T(8,128)(2,1)} %param.16), kind=kOutput, calls=%fused_computation.1 | convolution fusion | flops 268435456 | bytes 4849664 | tf_op jit(solution)/shard_map/dot_general | solution.py:329
  12.2 0.0 copy-done.5
  12.2 1.0 %copy.15.router_ref = bf16[2048,16]{1,0:T(8,128)(2,1)} copy(bf16[2048,16]{0,1:T(8,128)(2,1)S(1)} %copy-done.5) | data formatting | bytes 131072 | tf_op args[7]
  13.2 0.0 copy-done.4
  13.2 0.0 copy-start.3
  13.2 1.0 %copy-done.3 = f32[4,16,2048]{2,1,0:T(8,128)S(1)} copy-done((f32[4,16,2048]{2,1,0:T(8,128)S(1)}, f32[4,16,2048]{2,1,0:T(8,128)}, u32[]{:S(2)}) %copy-start.3) | copy-done | bytes 524312
  14.2 21.6 %gather_latent.1 = (bf16[4,2,2,16,2048]{4,3,2,1,0:T(8,128)(2,1)S(1)}, s32[4,64,8]{2,1,0:T(8,128)S(1)}) custom-call(f32[4,16,2048]{2,1,0:T(8,128)S(1)} %copy-done.3, f32[1,2048]{1,0:T(1,128)S(1)} %bitcast.17, s32[64,8]{1,0:T(8,128)S(1)} %copy.14.ids_ref), custom_call_target="tpu_custom_call" | custom-call | tf_op jit(solution)/shard_map/gather_latent/pallas_call | solution.py:128
  35.9 0.0 copy-start.1
  35.9 3.4 %copy-done.1 = bf16[4,512,2048]{2,1,0:T(8,128)(2,1)S(1)} copy-done((bf16[4,512,2048]{2,1,0:T(8,128)(2,1)S(1)}, bf16[4,512,2048]{2,1,0:T(8,128)(2,1)}, u32[]{:S(2)}) %copy-start.1) | copy-done | bytes 8388632
  39.2 0.0 copy-start.2
  39.2 1.0 %copy-done.2 = bf16[2048,16]{1,0:T(8,128)(2,1)S(1)} copy-done((bf16[2048,16]{1,0:T(8,128)(2,1)S(1)}, bf16[2048,16]{1,0:T(8,128)(2,1)}, u32[]{:S(2)}) %copy-start.2) | copy-done | bytes 65560
  40.3 21.4 %run_experts.1 = bf16[256,2048]{1,0:T(8,128)(2,1)S(1)} custom-call(bf16[256,2048]{1,0:T(8,128)(2,1)S(1)} %bitcast.15, s32[256,8]{1,0:T(8,128)S(1)} %bitcast.16, bf16[2048,16]{1,0:T(8,128)(2,1)S(1)} %copy-done.2, bf16[4,2048,2,512]{3,2,1,0:T(2,128)(2,1)} %right_ref.1, bf16[4,2048,2,512]{3,2,1,0:T(2,128)(2,1)} %right_ref.1, bf16[4,512,2048]{2,1,0:T(8,128)(2,1)S(1)} %copy-done.1), custom_call_target="tpu_custom_call" | custom-call | tf_op jit(solution)/shard_map/run_experts/pallas_call | solution.py:300
  61.7 19.3 %reduce_mixture.1 = bf16[2,2,16,2048]{3,2,1,0:T(8,128)(2,1)S(1)} custom-call(bf16[4,2,2,16,2048]{4,3,2,1,0:T(8,128)(2,1)S(1)} %bitcast.13), custom_call_target="tpu_custom_call" | custom-call | tf_op jit(solution)/shard_map/reduce_mixture/pallas_call | solution.py:231
  80.9 5.7 %convolution_convert_fusion = bf16[64,2048]{1,0:T(8,128)(2,1)} fusion(bf16[64,2048]{1,0:T(8,128)(2,1)S(1)} %bitcast.14, bf16[2048,2048]{1,0:T(8,128)(2,1)} %param.21), kind=kOutput, calls=%fused_computation.7 | convolution fusion | flops 537001984 | bytes 8912896 | tf_op jit(solution)/shard_map/dot_general | solution.py:335
Async XLA Ops:
  0.0 6.3 %copy-start = (bf16[64,96,2,128]{3,2,1,0:T(2,128)(2,1)S(1)}, bf16[64,96,2,128]{3,2,1,0:T(2,128)(2,1)}, u32[]{:S(2)}) copy-start(bf16[64,96,2,128]{3,2,1,0:T(2,128)(2,1)} %param.13) | copy-start | bytes 9437188
  8.2 3.9 %copy-start.5 = (bf16[2048,16]{0,1:T(8,128)(2,1)S(1)}, bf16[2048,16]{0,1:T(8,128)(2,1)}, u32[]{:S(2)}) copy-start(bf16[2048,16]{0,1:T(8,128)(2,1)} %param.18) | copy-start | bytes 196612
  8.3 4.9 %copy-start.4 = (f32[2048]{0:T(1024)S(1)}, f32[2048]{0:T(1024)}, u32[]{:S(2)}) copy-start(f32[2048]{0:T(1024)} %param.17) | copy-start | bytes 24580
  13.2 1.0 %copy-start.3 = (f32[4,16,2048]{2,1,0:T(8,128)S(1)}, f32[4,16,2048]{2,1,0:T(8,128)}, u32[]{:S(2)}) copy-start(f32[4,16,2048]{2,1,0:T(8,128)} %fusion.1.partial_ref) | copy-start | bytes 1572868
  35.9 3.4 %copy-start.1 = (bf16[4,512,2048]{2,1,0:T(8,128)(2,1)S(1)}, bf16[4,512,2048]{2,1,0:T(8,128)(2,1)}, u32[]{:S(2)}) copy-start(bf16[4,512,2048]{2,1,0:T(8,128)(2,1)} %down_ref.1) | copy-start | bytes 25165828
  39.2 1.0 %copy-start.2 = (bf16[2048,16]{1,0:T(8,128)(2,1)S(1)}, bf16[2048,16]{1,0:T(8,128)(2,1)}, u32[]{:S(2)}) copy-start(bf16[2048,16]{1,0:T(8,128)(2,1)} %copy.15.router_ref) | copy-start | bytes 196612
